TPU v7x, 128 devices: a whole 4x4x4 slice. The times are simulated.
128 devices in a mesh: row: 8 (over x, core), col: 16 (over z, y).
Axes of the slice: x: 4, y: 4, z: 4, core: 2. Of those that a mesh axis runs over, the one named last changes fastest.
Arguments:
- density: bfloat16 [6144, 6144], P('row', 'col'), may hold values from -5 to 5
- strips: bfloat16 [16384, 8, 128], P(('row', 'col')), may hold values from -5 to 5
- dest_device: int32 [16384, 1], P(('row', 'col')), may hold values from 0 to 127; in each aligned block of 128 rows (0 to 127, 128 to 255, ...) at most 2 rows name the same one
- atom_slot: int32 [16384], P(('row', 'col')), may hold values from 0 to 95
- block_slot: int32 [16384], P(('row', 'col')), may hold values from 0 to 2
- patterns: int32 [3, 48, 48], replicated, may hold values 0 or 1
Outputs:
- density_next: float32 [6144, 6144], P('row', 'col')
- response_next: float32 [6144, 6144], P('row', 'col')
Inputs may be any that keep to these rules, and one draw needn't show every extreme that they name: `dest_device`: of the 128 strips of one device, at most 2 name the same owner, and some owner is named that often.
All inputs are finite; a program needn't handle non-finite values.
Results may differ from a plain program's by a relative error of at most 0.0036.
Values may be sent and summed in bfloat16 or wider, within the bound.
A program may use at most 128 MiB of HBM per device.

v0:
```python
import math
import jax
import jax.numpy as jnp
from jax import lax
from jax.sharding import PartitionSpec as P

STEPS = 2
CAPACITY = 2


def tile_kept(patterns, which, row_offset, col_offset, block_rows, block_cols, block_width):
    window = lax.dynamic_slice(patterns[which], (row_offset, col_offset), (block_rows, block_cols))
    global_rows = row_offset + lax.iota(jnp.int32, block_rows)
    global_cols = col_offset + lax.iota(jnp.int32, block_cols)
    diagonal = (global_rows[:, None] == global_cols[None, :]).astype(jnp.int32)
    kept = jnp.maximum(window, diagonal).astype(jnp.float32)
    return jnp.repeat(jnp.repeat(kept, block_width, axis=0), block_width, axis=1)


def products(zeroth, linear):
    col_zero, col_first = (
        lax.all_gather(zeroth, "row", axis=0, tiled=True),
        lax.all_gather(linear, "row", axis=0, tiled=True),
    )
    pieces = (
        lax.all_gather(zeroth, "col", axis=1, tiled=True),
        lax.all_gather(linear, "col", axis=1, tiled=True),
    )
    square = jnp.dot(pieces[0], col_zero, preferred_element_type=jnp.float32)
    left_part = jnp.dot(pieces[0], col_first, preferred_element_type=jnp.float32)
    right_part = jnp.dot(pieces[1], col_zero, preferred_element_type=jnp.float32)
    return (square, left_part + right_part)


def on_device(density, strips, dest_device, atom_slot, block_slot, patterns):
    tile_rows, tile_cols = density.shape
    mesh_rows = lax.axis_size("row")
    mesh_cols = lax.axis_size("col")
    devices = mesh_rows * mesh_cols
    matrix_order = tile_rows * mesh_rows
    atom_width = strips.shape[1]
    block_width = strips.shape[2]
    block_rows = tile_rows // block_width
    block_cols = tile_cols // block_width
    row_offset = lax.axis_index("row") * block_rows
    col_offset = lax.axis_index("col") * block_cols
    kept_zero = tile_kept(patterns, 0, row_offset, col_offset, block_rows, block_cols, block_width)
    kept_first = tile_kept(patterns, 1, row_offset, col_offset, block_rows, block_cols, block_width)
    kept_field = tile_kept(patterns, 2, row_offset, col_offset, block_rows, block_cols, block_width)
    capacity = CAPACITY
    targets = dest_device[:, 0]
    order = lax.iota(jnp.int32, targets.shape[0])
    earlier = (targets[:, None] == targets[None, :]) & (order[None, :] < order[:, None])
    ranking = jnp.sum(earlier.astype(jnp.int32), axis=1)
    position = targets * capacity + ranking
    sent_strips = (
        jnp.zeros((devices * capacity, atom_width, block_width), strips.dtype)
        .at[position]
        .set(strips)
    )
    sent_atoms = jnp.full((devices * capacity,), -1, jnp.int32).at[position].set(atom_slot)
    sent_blocks = jnp.zeros((devices * capacity,), jnp.int32).at[position].set(block_slot)
    arrived = (
        lax.all_to_all(
            sent_strips.reshape(devices, capacity, atom_width, block_width),
            ("row", "col"),
            split_axis=0,
            concat_axis=0,
            tiled=True,
        ),
        lax.all_to_all(
            sent_atoms.reshape(devices, capacity),
            ("row", "col"),
            split_axis=0,
            concat_axis=0,
            tiled=True,
        ),
        lax.all_to_all(
            sent_blocks.reshape(devices, capacity),
            ("row", "col"),
            split_axis=0,
            concat_axis=0,
            tiled=True,
        ),
    )
    recv_strips = arrived[0].reshape(-1, atom_width * block_width)
    recv_atoms = arrived[1].reshape(-1)
    recv_blocks = arrived[2].reshape(-1)
    atoms_here = tile_rows // atom_width
    atom_match = recv_atoms[:, None] == lax.iota(jnp.int32, atoms_here)[None, :]
    block_match = recv_blocks[:, None] == lax.iota(jnp.int32, block_cols)[None, :]
    placing = (
        (atom_match[:, :, None] & block_match[:, None, :])
        .astype(jnp.bfloat16)
        .reshape(-1, atoms_here * block_cols)
    )
    summed = lax.dot_general(
        placing, recv_strips, (((0,), (0,)), ((), ())), preferred_element_type=jnp.float32
    )
    h_field = (
        summed.reshape(atoms_here, block_cols, atom_width, block_width)
        .transpose(0, 2, 1, 3)
        .reshape(tile_rows, tile_cols)
    )
    linear = (-(kept_field * h_field)).astype(jnp.bfloat16)
    zeroth = density
    inv_root = 1.0 / math.sqrt(matrix_order)
    new_zeroth = None
    new_linear = None
    for iteration in range(STEPS):
        square, crossed = products(zeroth, linear)
        if iteration % 2 == 0:
            new_zeroth = kept_zero * (square * inv_root)
            new_linear = kept_first * (crossed * inv_root)
        else:
            new_zeroth = kept_zero * (2.0 * zeroth.astype(jnp.float32) - square * inv_root)
            new_linear = kept_first * (2.0 * linear.astype(jnp.float32) - crossed * inv_root)
        zeroth = new_zeroth.astype(jnp.bfloat16)
        linear = new_linear.astype(jnp.bfloat16)
    return (new_zeroth, new_linear)


def solution(mesh):
    return jax.shard_map(
        on_device,
        mesh=mesh,
        in_specs=(
            P("row", "col"),
            P(("row", "col"), None, None),
            P(("row", "col"), None),
            P(("row", "col")),
            P(("row", "col")),
            P(),
        ),
        out_specs=(P("row", "col"), P("row", "col")),
        check_vma=False,
    )
```

profile of v0, /device:TPU:0, one launch (start us, length us, event | category | flops | bytes accessed | tf_op | source)
XLA Modules:
  0.0 540.9 jit_solution(16579620292933018582)
XLA Ops:
  7.2 0.7 all-gather.11.cloned.1.call-update
  7.9 0.9 convert_reduce_fusion
  8.8 0.7 fusion.18
  9.5 1.1 scatter_custom_fusion.1
  10.6 0.8 all_to_all.17
  11.4 11.1 %all-to-all-start.1 = ((s32[128,1,2]{2,1,0:T(1,128)}), s32[128,1,2]{2,1,0:T(1,128)S(1)}, u32[]{:S(2)}, u32[]{:S(2)}) async-start(s32[128,1,2]{2,1,0:T(1,128)} %bitcast.10), calls=%async_computation.1 | async-start | bytes 131072 | tf_op jit(solution)/shard_map/all_to_all | solution.py:78
  22.5 0.8 fusion.23
  23.4 0.1 copy.44
  23.9 1.1 scatter_custom_fusion
  25.0 0.8 all_to_all.15
  25.8 6.5 %all-to-all-done.1 = s32[128,1,2]{2,1,0:T(1,128)S(1)} async-done(((s32[128,1,2]{2,1,0:T(1,128)}), s32[128,1,2]{2,1,0:T(1,128)S(1)}, u32[]{:S(2)}, u32[]{:S(2)}) %all-to-all-start.1) | async-done | bytes 1056 | tf_op jit(solution)/shard_map/all_to_all | solution.py:78
  32.2 4.6 all-to-all-start
  36.9 0.9 broadcast_in_dim.50
  37.8 13.4 %scatter_fusion = bf16[256,8,128]{2,1,0:T(8,128)(2,1)} fusion(bf16[256,8,128]{2,1,0:T(8,128)(2,1)} %broadcast_in_dim.50, s32[128]{0:T(128)S(1)} %fusion.18, bf16[128,8,128]{2,1,0:T(8,128)(2,1)S(1)} %copy-done.2), kind=kCustom, calls=%fused_computation.2 | custom fusion | bytes 786944 | tf_op jit(solution)/shard_map/scatter | solution.py:59
  51.1 0.5 broadcast.64
  51.7 0.8 reduce.6
  52.5 0.1 eq.91
  52.6 9.7 %all-to-all-start.2 = ((bf16[128,2,8,128]{3,2,1,0:T(8,128)(2,1)}), bf16[128,2,8,128]{3,2,1,0:T(8,128)(2,1)S(1)}, u32[]{:S(2)}, u32[]{:S(2)}) async-start(bf16[128,2,8,128]{3,2,1,0:T(8,128)(2,1)} %bitcast.13), calls=%async_computation.2 | async-start | bytes 1048576 | tf_op jit(solution)/shard_map/all_to_all | solution.py:64
  62.4 0.8 reduce.7
  63.2 0.1 eq.87
  63.3 0.1 broadcast_and_fusion
  63.5 0.1 and.26
  63.7 12.2 %all-to-all-done.2 = bf16[128,2,8,128]{3,2,1,0:T(8,128)(2,1)S(1)} async-done(((bf16[128,2,8,128]{3,2,1,0:T(8,128)(2,1)}), bf16[128,2,8,128]{3,2,1,0:T(8,128)(2,1)S(1)}, u32[]{:S(2)}, u32[]{:S(2)}) %all-to-all-start.2) | async-done | bytes 524320 | tf_op jit(solution)/shard_map/all_to_all | solution.py:64
  76.0 0.2 copy.48
  76.2 0.4 convolution_bitcast_fusion.1
  76.6 0.7 copy.70
  77.3 0.4 copy.51
  77.7 0.9 fusion.12
  78.7 0.7 all-gather.17.cloned.1.call-update
  79.4 0.5 all-gather.9.cloned.1.call-update
  80.1 0.4 copy.54
  80.5 69.7 %all-gather.19.cloned.1.call-done = bf16[768,6144]{0,1:T(8,128)(2,1)} async-done(((bf16[768,384]{0,1:T(8,128)(2,1)}), bf16[768,6144]{0,1:T(8,128)(2,1)}) %all-gather.19.cloned.1.call-update) | async-done | bytes 9437200 | tf_op jit(solution)/shard_map/all_gather | solution.py:27
  150.2 9.0 %fusion.24 = f32[768,384]{1,0:T(8,128)S(1)} fusion(bf16[768,6144]{0,1:T(8,128)(2,1)} %all-gather.19.cloned.1.call-done, bf16[6144,384]{1,0:T(8,128)(2,1)} %all-gather.11.cloned.1.call-done), kind=kOutput, calls=%fused_computation.56 | convolution fusion | flops 3623878656 | bytes 15335424 | tf_op jit(solution)/shard_map/dot_general | solution.py:31
  159.3 27.1 %all-gather.17.cloned.1.call-done = bf16[6144,384]{0,1:T(8,128)(2,1)} async-done(((bf16[768,384]{0,1:T(8,128)(2,1)}), bf16[6144,384]{0,1:T(8,128)(2,1)}) %all-gather.17.cloned.1.call-update) | async-done | bytes 4718608 | tf_op jit(solution)/shard_map/all_gather | solution.py:23
  186.4 85.9 %all-gather.9.cloned.1.call-done = bf16[768,6144]{1,0:T(8,128)(2,1)} async-done(((bf16[768,384]{1,0:T(8,128)(2,1)}), bf16[768,6144]{1,0:T(8,128)(2,1)}) %all-gather.9.cloned.1.call-update) | async-done | bytes 9437200 | tf_op jit(solution)/shard_map/all_gather | solution.py:26
  272.2 9.8 %fusion.9 = bf16[768,384]{1,0:T(8,128)(2,1)} fusion(f32[768,384]{1,0:T(8,128)S(1)} %copy.54, f32[768,384]{1,0:T(8,128)S(1)} %fusion.24, bf16[6144,384]{0,1:T(8,128)(2,1)} %all-gather.17.cloned.1.call-done, bf16[768,6144]{1,0:T(8,128)(2,1)} %all-gather.9.cloned.1.call-done), kind=kOutput, calls=%fused_computation.17 | convolution fusion | flops 3625058304 | bytes 17104896 | tf_op jit(solution)/shard_map/dot_general | solution.py:30
  282.1 0.2 all-gather.13.cloned.1.call-start
  282.5 0.4 copy.43
  282.8 9.7 %fusion.10 = bf16[768,384]{1,0:T(8,128)(2,1)} fusion(f32[768,384]{1,0:T(8,128)S(1)} %copy.43, bf16[768,6144]{1,0:T(8,128)(2,1)} %all-gather.9.cloned.1.call-done, bf16[6144,384]{1,0:T(8,128)(2,1)} %all-gather.11.cloned.1.call-done), kind=kOutput, calls=%fused_computation.18 | convolution fusion | flops 3624763392 | bytes 15925248 | tf_op jit(solution)/shard_map/dot_general | solution.py:29
  292.6 0.7 all-gather.15.cloned.1.call-update
  293.4 0.7 all-gather.23.cloned.1.call-update
  294.1 21.6 %all-gather.21.cloned.1.call-done = bf16[6144,384]{1,0:T(8,128)(2,1)} async-done(((bf16[768,384]{1,0:T(8,128)(2,1)}), bf16[6144,384]{1,0:T(8,128)(2,1)}) %all-gather.21.cloned.1.call-update) | async-done | bytes 4718608 | tf_op jit(solution)/shard_map/all_gather | solution.py:23
  315.7 86.4 %all-gather.13.cloned.1.call-done = bf16[768,6144]{1,0:T(8,128)(2,1)} async-done(((bf16[768,384]{1,0:T(8,128)(2,1)}), bf16[768,6144]{1,0:T(8,128)(2,1)}) %all-gather.13.cloned.1.call-update) | async-done | bytes 9437200 | tf_op jit(solution)/shard_map/all_gather | solution.py:26
  402.2 9.8 %fusion.25 = f32[768,384]{1,0:T(8,128)} fusion(bf16[768,6144]{1,0:T(8,128)(2,1)} %all-gather.13.cloned.1.call-done, bf16[6144,384]{1,0:T(8,128)(2,1)} %all-gather.21.cloned.1.call-done), kind=kOutput, calls=%fused_computation.57 | convolution fusion | flops 3623878656 | bytes 15335424 | tf_op jit(solution)/shard_map/dot_general | solution.py:30
  411.9 26.0 %all-gather.15.cloned.1.call-done = bf16[6144,384]{1,0:T(8,128)(2,1)} async-done(((bf16[768,384]{1,0:T(8,128)(2,1)}), bf16[6144,384]{1,0:T(8,128)(2,1)}) %all-gather.15.cloned.1.call-update) | async-done | bytes 4718608 | tf_op jit(solution)/shard_map/all_gather | solution.py:22
  438.0 9.8 %fusion.2 = f32[768,384]{1,0:T(8,128)} fusion(f32[768,384]{1,0:T(8,128)S(1)} %copy.43, bf16[768,6144]{1,0:T(8,128)(2,1)} %all-gather.13.cloned.1.call-done, bf16[6144,384]{1,0:T(8,128)(2,1)} %all-gather.15.cloned.1.call-done, bf16[768,384]{1,0:T(8,128)(2,1)S(1)} %copy-done.1), kind=kOutput, calls=%fused_computation.9 | convolution fusion | flops 3625353216 | bytes 17104896 | tf_op jit(solution)/shard_map/dot_general | solution.py:29
  447.8 76.2 %all-gather.23.cloned.1.call-done = bf16[768,6144]{1,0:T(8,128)(2,1)} async-done(((bf16[768,384]{1,0:T(8,128)(2,1)}), bf16[768,6144]{1,0:T(8,128)(2,1)}) %all-gather.23.cloned.1.call-update) | async-done | bytes 9437200 | tf_op jit(solution)/shard_map/all_gather | solution.py:27
  524.0 10.1 %fusion.8 = f32[768,384]{1,0:T(8,128)} fusion(f32[768,384]{1,0:T(8,128)S(1)} %copy.54, f32[768,384]{1,0:T(8,128)} %fusion.25, bf16[768,6144]{1,0:T(8,128)(2,1)} %all-gather.23.cloned.1.call-done, bf16[6144,384]{1,0:T(8,128)(2,1)} %all-gather.15.cloned.1.call-done, bf16[768,384]{1,0:T(8,128)(2,1)S(1)} %copy-done), kind=kOutput, calls=%fused_computation.16 | convolution fusion | flops 3625648128 | bytes 18284544 | tf_op jit(solution)/shard_map/dot_general | solution.py:31
  (37 shorter events, 1.4 us)
Async XLA Ops:
  7.2 30.6 %copy-start.2 = (bf16[128,8,128]{2,1,0:T(8,128)(2,1)S(1)}, bf16[128,8,128]{2,1,0:T(8,128)(2,1)}, u32[]{:S(2)}) copy-start(bf16[128,8,128]{2,1,0:T(8,128)(2,1)} %param.7) | copy-start | bytes 786436
  7.2 73.4 %all-gather.11.cloned.1.call-start = ((), (), s32[]{:S(2)}) async-start(), calls=%async_computation.4 | async-start | bytes 5308416 | tf_op jit(solution)/shard_map/all_gather | solution.py:22
  11.4 20.8 %all-to-all-start.1 = ((s32[128,1,2]{2,1,0:T(1,128)}), s32[128,1,2]{2,1,0:T(1,128)S(1)}, u32[]{:S(2)}, u32[]{:S(2)}) async-start(s32[128,1,2]{2,1,0:T(1,128)} %bitcast.10), calls=%async_computation.1 | async-start | bytes 131072 | tf_op jit(solution)/shard_map/all_to_all | solution.py:78
  32.2 20.4 %all-to-all-start = ((s32[128,1,2]{2,1,0:T(1,128)}), s32[128,1,2]{2,1,0:T(1,128)S(1)}, u32[]{:S(2)}, u32[]{:S(2)}) async-start(s32[128,1,2]{2,1,0:T(1,128)} %bitcast.9), calls=%async_computation | async-start | bytes 131072 | tf_op jit(solution)/shard_map/all_to_all | solution.py:71
  52.6 23.3 %all-to-all-start.2 = ((bf16[128,2,8,128]{3,2,1,0:T(8,128)(2,1)}), bf16[128,2,8,128]{3,2,1,0:T(8,128)(2,1)S(1)}, u32[]{:S(2)}, u32[]{:S(2)}) async-start(bf16[128,2,8,128]{3,2,1,0:T(8,128)(2,1)} %bitcast.13), calls=%async_computation.2 | async-start | bytes 1048576 | tf_op jit(solution)/shard_map/all_to_all | solution.py:64
  62.3 87.9 %all-gather.19.cloned.1.call-start = ((), (), s32[]{:S(2)}) async-start(), calls=%async_computation.8 | async-start | bytes 10027008 | tf_op jit(solution)/shard_map/all_gather | solution.py:27
  78.6 107.8 %all-gather.17.cloned.1.call-start = ((), (), s32[]{:S(2)}) async-start(), calls=%async_computation.7 | async-start | bytes 5308416 | tf_op jit(solution)/shard_map/all_gather | solution.py:23
  79.3 192.9 %all-gather.9.cloned.1.call-start = ((), (), s32[]{:S(2)}) async-start(), calls=%async_computation.3 | async-start | bytes 10027008 | tf_op jit(solution)/shard_map/all_gather | solution.py:26
  79.9 235.8 %all-gather.21.cloned.1.call-start = ((), (), s32[]{:S(2)}) async-start(), calls=%async_computation.9 | async-start | bytes 5308416 | tf_op jit(solution)/shard_map/all_gather | solution.py:23
  282.1 120.1 %all-gather.13.cloned.1.call-start = ((), (), s32[]{:S(2)}) async-start(), calls=%async_computation.5 | async-start | bytes 10027008 | tf_op jit(solution)/shard_map/all_gather | solution.py:26
  292.6 145.4 %all-gather.15.cloned.1.call-start = ((), (), s32[]{:S(2)}) async-start(), calls=%async_computation.6 | async-start | bytes 5308416 | tf_op jit(solution)/shard_map/all_gather | solution.py:22
  293.3 230.6 %all-gather.23.cloned.1.call-start = ((), (), s32[]{:S(2)}) async-start(), calls=%async_computation.10 | async-start | bytes 10027008 | tf_op jit(solution)/shard_map/all_gather | solution.py:27
  294.1 143.9 %copy-start.1 = (bf16[768,384]{1,0:T(8,128)(2,1)S(1)}, bf16[768,384]{1,0:T(8,128)(2,1)}, u32[]{:S(2)}) copy-start(bf16[768,384]{1,0:T(8,128)(2,1)} %fusion.10) | copy-start | bytes 1769476
  411.9 112.0 %copy-start = (bf16[768,384]{1,0:T(8,128)(2,1)S(1)}, bf16[768,384]{1,0:T(8,128)(2,1)}, u32[]{:S(2)}) copy-start(bf16[768,384]{1,0:T(8,128)(2,1)} %fusion.9) | copy-start | bytes 1769476
Sparse Core Ops, SparseCore 0:
  9.7 37.7 all-gather.10
  78.7 71.4 all-gather.18
  152.5 33.8 all-gather.16
  188.4 83.8 all-gather.8
  282.2 33.4 all-gather.20
  318.3 83.8 all-gather.12
  404.4 33.4 all-gather.14
  440.1 83.8 all-gather.22
where the time goes:
time: 541 us
  waiting for transfers between devices  415 us (77%)
  matrix products  58.5 us (11%)
  starting transfers between devices  25.9 us (5%)
  local copies, waits for them, and re-layouts  22.8 us (4%)
  between operations  14.4 us (3%)
    all_gather x2, waiting for transfers between devices, products(): lax.all_gather(zeroth, 'col', axis=1, tiled=True)  172 us
    all_gather x2, waiting for transfers between devices, products(): lax.all_gather(linear, 'col', axis=1, tiled=True)  146 us
    all_gather x2, waiting for transfers between devices, products(): lax.all_gather(linear, 'row', axis=0, tiled=True)  48.8 us
    all_gather x2, waiting for transfers between devices, products(): lax.all_gather(zeroth, 'row', axis=0, tiled=True)  26 us
    dot_general x2, matrix products, products(): jnp.dot(pieces[0], col_first, preferred_element_type=jnp.float32)  19.6 us
    dot_general x2, matrix products, products(): square = jnp.dot(pieces[0], col_zero, preferred_element_type=jnp.float32)  19.5 us
    dot_general x2, matrix products, products(): jnp.dot(pieces[1], col_zero, preferred_element_type=jnp.float32)  19.1 us
    scatter x1, local copies, waits for them, and re-layouts, on_device(): sent_strips = jnp.zeros((devices * capacity, atom_width, block_width), st...  13.4 us
  transfers between devices with their start and end apart: 11, of which 9 were waited for; matrix products, arithmetic and copies ran while one was open for 12% of the time, Pallas kernels for 0%

commit v1 on v0

--- a/solution.py
+++ b/solution.py
@@ -6,6 +6,27 @@
 
 STEPS = 2
 CAPACITY = 2
+
+
+def gather_around(x, axis, dim):
+    size, index, rows = (lax.axis_size(axis), lax.axis_index(axis), x.shape[dim])
+    right = [(i, (i + 1) % size) for i in range(size)]
+    downward = [(i, (i - 1) % size) for i in range(size)]
+    out = jnp.zeros((*x.shape[:dim], size * rows, *x.shape[dim + 1 :]), x.dtype)
+    out = lax.dynamic_update_slice_in_dim(out, x, index * rows, axis=dim)
+    from_left = from_right = x
+    half = size // 2
+    for step in range(1, half + 1):
+        from_left = lax.ppermute(from_left, axis, right)
+        out = lax.dynamic_update_slice_in_dim(
+            out, from_left, (index - step) % size * rows, axis=dim
+        )
+        if step < size - half:
+            from_right = lax.ppermute(from_right, axis, downward)
+            out = lax.dynamic_update_slice_in_dim(
+                out, from_right, (index + step) % size * rows, axis=dim
+            )
+    return out
 
 
 def tile_kept(patterns, which, row_offset, col_offset, block_rows, block_cols, block_width):
@@ -20,7 +41,7 @@
 def products(zeroth, linear):
     col_zero, col_first = (
         lax.all_gather(zeroth, "row", axis=0, tiled=True),
-        lax.all_gather(linear, "row", axis=0, tiled=True),
+        gather_around(linear, "row", 0),
     )
     pieces = (
         lax.all_gather(zeroth, "col", axis=1, tiled=True),

time: 541 us -> 454 us (0.84)
  waiting for transfers between devices: 415 us -> 283 us
  local copies, waits for them, and re-layouts: 22.8 us -> 49.6 us
  starting transfers between devices: 25.9 us -> 44.1 us
    all_gather x2, waiting for transfers between devices: 172 us -> 112 us  [products(): lax.all_gather(zeroth, 'col', axis=1, tiled=True)]
    ppermute x0 -> x14, waiting for transfers between devices: none -> 52.4 us  [the longest x8 52.4 us: gather_around(): from_left = lax.ppermute(from_left, axis, right)]
    all_gather x2 -> x0, waiting for transfers between devices: 48.8 us -> none  [products(): lax.all_gather(linear, 'row', axis=0, tiled=True)]
    all_gather x2, waiting for transfers between devices: 146 us -> 98.6 us  [products(): lax.all_gather(linear, 'col', axis=1, tiled=True)]
    all_gather x2, waiting for transfers between devices: 26 us -> 0.02 us  [products(): lax.all_gather(zeroth, 'row', axis=0, tiled=True)]
    ppermute x0 -> x14, starting transfers between devices: none -> 18.2 us  [the longest x6 18.1 us: gather_around(): from_right = lax.ppermute(from_right, axis, downward)]
    dynamic_update_slice x0 -> x15, local copies, waits for them, and re-layouts: none -> 13.4 us  [the longest x8 7.13 us: gather_around(): lax.dynamic_update_slice_in_dim(out, from_left, (index - step) % size * r...]
    ppermute x0 -> x7, local copies, waits for them, and re-layouts: none -> 6.41 us  [the longest x3 4.11 us: gather_around(): from_right = lax.ppermute(from_right, axis, downward)]
  transfers between devices with their start and end apart: 11 -> 23, of which waited for: 9 -> 13; matrix products, arithmetic and copies ran while one was open for 12% -> 20% of each run, Pallas kernels for 0% -> 0%
where the time goes in v1:
time: 454 us; the launch traced here: 453 us
  waiting for transfers between devices  283 us (62%)
  matrix products  57 us (13%)
  local copies, waits for them, and re-layouts  49.6 us (11%)
  starting transfers between devices  44.1 us (10%)
  between operations  14.4 us (3%)
    all_gather x2, waiting for transfers between devices, products(): lax.all_gather(zeroth, 'col', axis=1, tiled=True)  112 us
    all_gather x2, waiting for transfers between devices, products(): lax.all_gather(linear, 'col', axis=1, tiled=True)  98.6 us
    ppermute x8, waiting for transfers between devices, gather_around(): from_left = lax.ppermute(from_left, axis, right)  52.4 us
    dot_general x2, matrix products, products(): square = jnp.dot(pieces[0], col_zero, preferred_element_type=jnp.float32)  19.5 us
    dot_general x2, matrix products, products(): jnp.dot(pieces[0], col_first, preferred_element_type=jnp.float32)  18.8 us
    dot_general x2, matrix products, products(): jnp.dot(pieces[1], col_zero, preferred_element_type=jnp.float32)  18.4 us
    ppermute x6, starting transfers between devices, gather_around(): from_right = lax.ppermute(from_right, axis, downward)  18.1 us
    scatter x1, local copies, waits for them, and re-layouts, on_device(): sent_strips = jnp.zeros((devices * capacity, atom_width, block_width), st...  14 us
  transfers between devices with their start and end apart: 23, of which 13 were waited for; matrix products, arithmetic and copies ran while one was open for 20% of the time, Pallas kernels for 0%

profile of v1, /device:TPU:0, one launch (start us, length us, event | category | flops | bytes accessed | tf_op | source)
XLA Modules:
  0.0 452.6 jit_solution(7118370819507254357)
XLA Ops:
  8.6 0.9 convert_reduce_fusion
  10.2 1.1 scatter_custom_fusion.1
  12.1 11.1 %all-to-all-start.1 = ((s32[128,1,2]{2,1,0:T(1,128)}), s32[128,1,2]{2,1,0:T(1,128)S(1)}, u32[]{:S(2)}, u32[]{:S(2)}) async-start(s32[128,1,2]{2,1,0:T(1,128)} %bitcast.10), calls=%async_computation.1 | async-start | bytes 131072 | tf_op jit(solution)/shard_map/all_to_all | solution.py:99
  24.6 1.1 scatter_custom_fusion
  26.5 6.2 %all-to-all-done.1 = s32[128,1,2]{2,1,0:T(1,128)S(1)} async-done(((s32[128,1,2]{2,1,0:T(1,128)}), s32[128,1,2]{2,1,0:T(1,128)S(1)}, u32[]{:S(2)}, u32[]{:S(2)}) %all-to-all-start.1) | async-done | bytes 1056 | tf_op jit(solution)/shard_map/all_to_all | solution.py:99
  32.7 4.6 %all-to-all-start = ((s32[128,1,2]{2,1,0:T(1,128)}), s32[128,1,2]{2,1,0:T(1,128)S(1)}, u32[]{:S(2)}, u32[]{:S(2)}) async-start(s32[128,1,2]{2,1,0:T(1,128)} %bitcast.9), calls=%async_computation | async-start | bytes 131072 | tf_op jit(solution)/shard_map/all_to_all | solution.py:92
  38.2 14.0 %scatter_fusion = bf16[256,8,128]{2,1,0:T(8,128)(2,1)} fusion(bf16[256,8,128]{2,1,0:T(8,128)(2,1)} %broadcast_in_dim.50, s32[128]{0:T(128)S(1)} %fusion.18, bf16[128,8,128]{2,1,0:T(8,128)(2,1)} %param.7), kind=kCustom, calls=%fused_computation.2 | custom fusion | bytes 786944 | tf_op jit(solution)/shard_map/scatter | solution.py:80
  53.6 9.8 %all-to-all-start.2 = ((bf16[128,2,8,128]{3,2,1,0:T(8,128)(2,1)}), bf16[128,2,8,128]{3,2,1,0:T(8,128)(2,1)S(1)}, u32[]{:S(2)}, u32[]{:S(2)}) async-start(bf16[128,2,8,128]{3,2,1,0:T(8,128)(2,1)} %bitcast.13), calls=%async_computation.2 | async-start | bytes 1048576 | tf_op jit(solution)/shard_map/all_to_all | solution.py:85
  64.8 12.2 %all-to-all-done.2 = bf16[128,2,8,128]{3,2,1,0:T(8,128)(2,1)S(1)} async-done(((bf16[128,2,8,128]{3,2,1,0:T(8,128)(2,1)}), bf16[128,2,8,128]{3,2,1,0:T(8,128)(2,1)S(1)}, u32[]{:S(2)}, u32[]{:S(2)}) %all-to-all-start.2) | async-done | bytes 524320 | tf_op jit(solution)/shard_map/all_to_all | solution.py:85
  78.8 0.9 fusion.12
  80.4 58.2 %all-gather.7.cloned.1.call-done = bf16[768,6144]{1,0:T(8,128)(2,1)} async-done(((bf16[768,384]{1,0:T(8,128)(2,1)}), bf16[768,6144]{1,0:T(8,128)(2,1)}) %all-gather.7.cloned.1.call-update) | async-done | bytes 9437200 | tf_op jit(solution)/shard_map/all_gather | solution.py:47
  138.6 9.7 %fusion.10 = bf16[768,384]{1,0:T(8,128)(2,1)} fusion(f32[768,384]{1,0:T(8,128)S(1)} %copy.59, bf16[768,6144]{1,0:T(8,128)(2,1)} %all-gather.7.cloned.1.call-done, bf16[6144,384]{1,0:T(8,128)(2,1)} %all-gather.9.cloned.1.call-done), kind=kOutput, calls=%fused_computation.18 | convolution fusion | flops 3624763392 | bytes 15925248 | tf_op jit(solution)/shard_map/dot_general | solution.py:50
  149.2 2.9 collective-permute-start.1
  152.1 7.6 %collective-permute-done = bf16[768,384]{0,1:T(8,128)(2,1)S(1)} collective-permute-done((bf16[768,384]{0,1:T(8,128)(2,1)S(1)}, bf16[768,384]{0,1:T(8,128)(2,1)S(1)}, u32[]{:S(2)}, u32[]{:S(2)}) %collective-permute-start) | collective-permute-done | bytes 589856 | tf_op jit(solution)/shard_map/ppermute | solution.py:20
  159.7 3.3 collective-permute-start.3
  163.0 7.3 %collective-permute-done.2 = bf16[768,384]{0,1:T(8,128)(2,1)} collective-permute-done((bf16[768,384]{0,1:T(8,128)(2,1)S(1)}, bf16[768,384]{0,1:T(8,128)(2,1)}, u32[]{:S(2)}, u32[]{:S(2)}) %collective-permute-start.2) | collective-permute-done | bytes 589856 | tf_op jit(solution)/shard_map/ppermute | solution.py:20
  170.5 1.4 copy.78
  172.2 3.0 collective-permute-start.5
  175.2 2.5 broadcast.58.clone
  177.7 0.9 constant_dynamic-update-slice_fusion.15
  178.9 1.4 copy.70
  181.2 0.9 constant_dynamic-update-slice_fusion.13
  182.1 1.4 copy.71
  183.5 1.4 copy.72
  184.9 0.9 constant_dynamic-update-slice_fusion.12
  187.0 1.4 copy.74
  188.3 0.9 constant_dynamic-update-slice_fusion.10
  189.2 0.9 constant_dynamic-update-slice_fusion.9
  190.2 1.5 collective-permute-done.6
  192.9 22.8 %all-gather.15.cloned.1.call-done = bf16[768,6144]{0,1:T(8,128)(2,1)} async-done(((bf16[768,384]{0,1:T(8,128)(2,1)}), bf16[768,6144]{0,1:T(8,128)(2,1)}) %all-gather.15.cloned.1.call-update) | async-done | bytes 9437200 | tf_op jit(solution)/shard_map/all_gather | solution.py:48
  215.7 9.0 %fusion.24 = f32[768,384]{1,0:T(8,128)S(1)} fusion(bf16[768,6144]{0,1:T(8,128)(2,1)} %all-gather.15.cloned.1.call-done, bf16[6144,384]{1,0:T(8,128)(2,1)} %all-gather.9.cloned.1.call-done), kind=kOutput, calls=%fused_computation.72 | convolution fusion | flops 3623878656 | bytes 15335424 | tf_op jit(solution)/shard_map/dot_general | solution.py:52
  224.8 2.6 broadcast.58
  227.3 10.3 %constant_dynamic-update-slice_fusion.7 = (bf16[6144,384]{1,0:T(8,128)(2,1)}, bf16[768,384]{1,0:T(8,128)(2,1)}) fusion(bf16[6144,384]{1,0:T(8,128)(2,1)} %broadcast.58, s32[]{:T(128)S(6)} %select_n.96, f32[768,384]{1,0:T(8,128)S(1)} %copy-done.2, f32[768,384]{1,0:T(8,128)S(1)} %fusion.24, bf16[768,6144]{1,0:T(8,128)(2,1)} %all-gather.7.cloned.1.call-done, ...), kind=kOutput, calls=%fused_computation.43 | convolution fusion | flops 3625058304 | bytes 17694724 | tf_op jit(solution)/shard_map/dot_general | solution.py:51
  237.7 2.9 collective-permute-start.8
  240.6 15.7 %collective-permute-done.7 = bf16[768,384]{1,0:T(8,128)(2,1)S(1)} collective-permute-done((bf16[768,384]{1,0:T(8,128)(2,1)}, bf16[768,384]{1,0:T(8,128)(2,1)S(1)}, u32[]{:S(2)}, u32[]{:S(2)}) %collective-permute-start.7) | collective-permute-done | bytes 589856 | tf_op jit(solution)/shard_map/ppermute | solution.py:20
  256.4 3.0 collective-permute-start.10
  259.3 7.6 %collective-permute-done.9 = bf16[768,384]{1,0:T(8,128)(2,1)S(1)} collective-permute-done((bf16[768,384]{1,0:T(8,128)(2,1)S(1)}, bf16[768,384]{1,0:T(8,128)(2,1)S(1)}, u32[]{:S(2)}, u32[]{:S(2)}) %collective-permute-start.9) | collective-permute-done | bytes 589856 | tf_op jit(solution)/shard_map/ppermute | solution.py:20
  266.9 3.0 collective-permute-start.12
  269.8 0.9 constant_dynamic-update-slice_fusion.6
  270.7 6.7 %collective-permute-done.11 = bf16[768,384]{1,0:T(8,128)(2,1)S(1)} collective-permute-done((bf16[768,384]{1,0:T(8,128)(2,1)S(1)}, bf16[768,384]{1,0:T(8,128)(2,1)S(1)}, u32[]{:S(2)}, u32[]{:S(2)}) %collective-permute-start.11) | collective-permute-done | bytes 589856 | tf_op jit(solution)/shard_map/ppermute | solution.py:20
  277.4 0.9 constant_dynamic-update-slice_fusion.5
  278.3 0.9 constant_dynamic-update-slice_fusion.4
  281.8 6.1 %collective-permute-done.13 = bf16[768,384]{1,0:T(8,128)(2,1)S(1)} collective-permute-done((bf16[768,384]{1,0:T(8,128)(2,1)S(1)}, bf16[768,384]{1,0:T(8,128)(2,1)S(1)}, u32[]{:S(2)}, u32[]{:S(2)}) %collective-permute-start.13) | collective-permute-done | bytes 589856 | tf_op jit(solution)/shard_map/ppermute | solution.py:20
  288.8 53.4 %all-gather.11.cloned.1.call-done = bf16[768,6144]{1,0:T(8,128)(2,1)} async-done(((bf16[768,384]{1,0:T(8,128)(2,1)}), bf16[768,6144]{1,0:T(8,128)(2,1)}) %all-gather.11.cloned.1.call-update) | async-done | bytes 9437200 | tf_op jit(solution)/shard_map/all_gather | solution.py:47
  342.2 9.8 %fusion.2 = f32[768,384]{1,0:T(8,128)} fusion(f32[768,384]{1,0:T(8,128)S(1)} %copy.59, bf16[768,6144]{1,0:T(8,128)(2,1)} %all-gather.11.cloned.1.call-done, bf16[6144,384]{1,0:T(8,128)(2,1)} %all-gather.13.cloned.1.call-done, bf16[768,384]{1,0:T(8,128)(2,1)S(1)} %copy-done.1), kind=kOutput, calls=%fused_computation.9 | convolution fusion | flops 3625353216 | bytes 17104896 | tf_op jit(solution)/shard_map/dot_general | solution.py:50
  352.1 75.8 %all-gather.17.cloned.1.call-done = bf16[768,6144]{1,0:T(8,128)(2,1)} async-done(((bf16[768,384]{1,0:T(8,128)(2,1)}), bf16[768,6144]{1,0:T(8,128)(2,1)}) %all-gather.17.cloned.1.call-update) | async-done | bytes 9437200 | tf_op jit(solution)/shard_map/all_gather | solution.py:48
  427.9 9.3 %fusion.25 = f32[768,384]{1,0:T(8,128)S(1)} fusion(bf16[768,6144]{1,0:T(8,128)(2,1)} %all-gather.17.cloned.1.call-done, bf16[6144,384]{1,0:T(8,128)(2,1)} %all-gather.13.cloned.1.call-done), kind=kOutput, calls=%fused_computation.73 | convolution fusion | flops 3623878656 | bytes 15335424 | tf_op jit(solution)/shard_map/dot_general | solution.py:52
  437.2 8.5 %fusion.8 = f32[768,384]{1,0:T(8,128)} fusion(f32[768,384]{1,0:T(8,128)S(1)} %copy-done.2, f32[768,384]{1,0:T(8,128)S(1)} %fusion.25, bf16[768,6144]{1,0:T(8,128)(2,1)S(1)} %copy-done.6, bf16[6144,384]{1,0:T(8,128)(2,1)} %constant_dynamic-update-slice_fusion, bf16[768,384]{1,0:T(8,128)(2,1)S(1)} %copy-done.5), kind=kOutput, calls=%fused_computation.16 | convolution fusion | flops 3625648128 | bytes 18284544 | tf_op jit(solution)/shard_map/dot_general | solution.py:51
  (92 shorter events, 19.4 us)
Async XLA Ops:
  7.2 73.2 %all-gather.9.cloned.1.call-start = ((), (), s32[]{:S(2)}) async-start(), calls=%async_computation.4 | async-start | bytes 5308416 | tf_op jit(solution)/shard_map/all_gather | solution.py:43
  7.9 130.7 %all-gather.7.cloned.1.call-start = ((), (), s32[]{:S(2)}) async-start(), calls=%async_computation.3 | async-start | bytes 10027008 | tf_op jit(solution)/shard_map/all_gather | solution.py:47
  12.1 20.6 %all-to-all-start.1 = ((s32[128,1,2]{2,1,0:T(1,128)}), s32[128,1,2]{2,1,0:T(1,128)S(1)}, u32[]{:S(2)}, u32[]{:S(2)}) async-start(s32[128,1,2]{2,1,0:T(1,128)} %bitcast.10), calls=%async_computation.1 | async-start | bytes 131072 | tf_op jit(solution)/shard_map/all_to_all | solution.py:99
  32.7 21.0 %all-to-all-start = ((s32[128,1,2]{2,1,0:T(1,128)}), s32[128,1,2]{2,1,0:T(1,128)S(1)}, u32[]{:S(2)}, u32[]{:S(2)}) async-start(s32[128,1,2]{2,1,0:T(1,128)} %bitcast.9), calls=%async_computation | async-start | bytes 131072 | tf_op jit(solution)/shard_map/all_to_all | solution.py:92
  53.6 23.4 %all-to-all-start.2 = ((bf16[128,2,8,128]{3,2,1,0:T(8,128)(2,1)}), bf16[128,2,8,128]{3,2,1,0:T(8,128)(2,1)S(1)}, u32[]{:S(2)}, u32[]{:S(2)}) async-start(bf16[128,2,8,128]{3,2,1,0:T(8,128)(2,1)} %bitcast.13), calls=%async_computation.2 | async-start | bytes 1048576 | tf_op jit(solution)/shard_map/all_to_all | solution.py:85
  63.4 152.3 %all-gather.15.cloned.1.call-start = ((), (), s32[]{:S(2)}) async-start(), calls=%async_computation.7 | async-start | bytes 10027008 | tf_op jit(solution)/shard_map/all_gather | solution.py:48
  79.8 209.0 %all-gather.13.cloned.1.call-start = ((), (), s32[]{:S(2)}) async-start(), calls=%async_computation.6 | async-start | bytes 5308416 | tf_op jit(solution)/shard_map/all_gather | solution.py:43
  80.3 68.8 %copy-start = (bf16[768,384]{0,1:T(8,128)(2,1)S(1)}, bf16[768,384]{0,1:T(8,128)(2,1)}, u32[]{:S(2)}) copy-start(bf16[768,384]{0,1:T(8,128)(2,1)} %fusion.12) | copy-start | bytes 1769476
  148.3 193.9 %all-gather.11.cloned.1.call-start = ((), (), s32[]{:S(2)}) async-start(), calls=%async_computation.5 | async-start | bytes 10027008 | tf_op jit(solution)/shard_map/all_gather | solution.py:47
  148.9 279.0 %all-gather.17.cloned.1.call-start = ((), (), s32[]{:S(2)}) async-start(), calls=%async_computation.8 | async-start | bytes 10027008 | tf_op jit(solution)/shard_map/all_gather | solution.py:48
  149.2 10.5 %collective-permute-start = (bf16[768,384]{0,1:T(8,128)(2,1)S(1)}, bf16[768,384]{0,1:T(8,128)(2,1)S(1)}, u32[]{:S(2)}, u32[]{:S(2)}) collective-permute-start(bf16[768,384]{0,1:T(8,128)(2,1)S(1)} %copy-done), channel_id=1, source_target_pairs={{0,16},{16,32},{32,48},{48,64},{64,80},{80,96},{96,112},{112,0},{1... | collective-permute-start | bytes 1769480 | tf_op jit(solution)/shard_map/ppermute | solution.py:20
  149.2 10.5 %collective-permute-start.1 = (bf16[768,384]{0,1:T(8,128)(2,1)S(1)}, bf16[768,384]{0,1:T(8,128)(2,1)}, u32[]{:S(2)}, u32[]{:S(2)}) collective-permute-start(bf16[768,384]{0,1:T(8,128)(2,1)S(1)} %copy-done), channel_id=1, source_target_pairs={{0,112},{16,0},{32,16},{48,32},{64,48},{80,64},{96,80},{112,96},{1... | collective-permute-start | bytes 1769480 | tf_op jit(solution)/shard_map/ppermute | solution.py:25
  159.7 10.7 %copy-start.3 = (bf16[768,384]{0,1:T(8,128)(2,1)}, bf16[768,384]{0,1:T(8,128)(2,1)S(1)}, u32[]{:S(2)}) copy-start(bf16[768,384]{0,1:T(8,128)(2,1)S(1)} %collective-permute-done) | copy-start | bytes 1769476
  159.7 10.6 %collective-permute-start.2 = (bf16[768,384]{0,1:T(8,128)(2,1)S(1)}, bf16[768,384]{0,1:T(8,128)(2,1)}, u32[]{:S(2)}, u32[]{:S(2)}) collective-permute-start(bf16[768,384]{0,1:T(8,128)(2,1)S(1)} %collective-permute-done), channel_id=1, source_target_pairs={{0,16},{16,32},{32,48},{48,64},{64,80},{80,96},{96,112},{112,0},{1... | collective-permute-start | bytes 1769480 | tf_op jit(solution)/shard_map/ppermute | solution.py:20
  159.7 12.5 %collective-permute-start.3 = (bf16[768,384]{0,1:T(8,128)(2,1)}, bf16[768,384]{0,1:T(8,128)(2,1)}, u32[]{:S(2)}, u32[]{:S(2)}) collective-permute-start(bf16[768,384]{0,1:T(8,128)(2,1)} %collective-permute-done.1), channel_id=1, source_target_pairs={{0,112},{16,0},{32,16},{48,32},{64,48},{80,64},{96,80},{112,96},{1... | collective-permute-start | bytes 1769480 | tf_op jit(solution)/shard_map/ppermute | solution.py:25
  170.3 10.9 %collective-permute-start.4 = (bf16[768,384]{0,1:T(8,128)(2,1)}, bf16[768,384]{0,1:T(8,128)(2,1)S(1)}, u32[]{:S(2)}, u32[]{:S(2)}) collective-permute-start(bf16[768,384]{0,1:T(8,128)(2,1)} %collective-permute-done.2), channel_id=1, source_target_pairs={{0,16},{16,32},{32,48},{48,64},{64,80},{80,96},{96,112},{112,0},{1... | collective-permute-start | bytes 1769480 | tf_op jit(solution)/shard_map/ppermute | solution.py:20
  171.9 6.7 %copy-start.4 = (bf16[768,384]{0,1:T(8,128)(2,1)S(1)}, bf16[768,384]{0,1:T(8,128)(2,1)}, u32[]{:S(2)}) copy-start(bf16[768,384]{0,1:T(8,128)(2,1)} %copy-done.3) | copy-start | bytes 1769476
  172.2 14.8 %collective-permute-start.5 = (bf16[768,384]{0,1:T(8,128)(2,1)}, bf16[768,384]{0,1:T(8,128)(2,1)}, u32[]{:S(2)}, u32[]{:S(2)}) collective-permute-start(bf16[768,384]{0,1:T(8,128)(2,1)} %collective-permute-done.3), channel_id=1, source_target_pairs={{0,112},{16,0},{32,16},{48,32},{64,48},{80,64},{96,80},{112,96},{1... | collective-permute-start | bytes 1769480 | tf_op jit(solution)/shard_map/ppermute | solution.py:25
  181.2 10.5 %collective-permute-start.6 = (bf16[768,384]{0,1:T(8,128)(2,1)S(1)}, bf16[768,384]{0,1:T(8,128)(2,1)S(1)}, u32[]{:S(2)}, u32[]{:S(2)}) collective-permute-start(bf16[768,384]{0,1:T(8,128)(2,1)S(1)} %collective-permute-done.4), channel_id=1, source_target_pairs={{0,16},{16,32},{32,48},{48,64},{64,80},{80,96},{96,112},{112,0},{1... | collective-permute-start | bytes 1769480 | tf_op jit(solution)/shard_map/ppermute | solution.py:20
  224.7 2.6 copy-start.2
  237.6 104.6 %copy-start.1 = (bf16[768,384]{1,0:T(8,128)(2,1)S(1)}, bf16[768,384]{1,0:T(8,128)(2,1)}, u32[]{:S(2)}) copy-start(bf16[768,384]{1,0:T(8,128)(2,1)} %fusion.10) | copy-start | bytes 1769476
  237.6 18.7 %collective-permute-start.7 = (bf16[768,384]{1,0:T(8,128)(2,1)}, bf16[768,384]{1,0:T(8,128)(2,1)S(1)}, u32[]{:S(2)}, u32[]{:S(2)}) collective-permute-start(bf16[768,384]{1,0:T(8,128)(2,1)} %get-tuple-element.9), channel_id=1, source_target_pairs={{0,16},{16,32},{32,48},{48,64},{64,80},{80,96},{96,112},{112,0},{1... | collective-permute-start | bytes 1769480 | tf_op jit(solution)/shard_map/ppermute | solution.py:20
  237.7 18.7 %collective-permute-start.8 = (bf16[768,384]{1,0:T(8,128)(2,1)}, bf16[768,384]{1,0:T(8,128)(2,1)S(1)}, u32[]{:S(2)}, u32[]{:S(2)}) collective-permute-start(bf16[768,384]{1,0:T(8,128)(2,1)} %get-tuple-element.9), channel_id=1, source_target_pairs={{0,112},{16,0},{32,16},{48,32},{64,48},{80,64},{96,80},{112,96},{1... | collective-permute-start | bytes 1769480 | tf_op jit(solution)/shard_map/ppermute | solution.py:25
  256.3 10.5 %collective-permute-start.9 = (bf16[768,384]{1,0:T(8,128)(2,1)S(1)}, bf16[768,384]{1,0:T(8,128)(2,1)S(1)}, u32[]{:S(2)}, u32[]{:S(2)}) collective-permute-start(bf16[768,384]{1,0:T(8,128)(2,1)S(1)} %collective-permute-done.7), channel_id=1, source_target_pairs={{0,16},{16,32},{32,48},{48,64},{64,80},{80,96},{96,112},{112,0},{1... | collective-permute-start | bytes 1769480 | tf_op jit(solution)/shard_map/ppermute | solution.py:20
  256.4 10.5 %collective-permute-start.10 = (bf16[768,384]{1,0:T(8,128)(2,1)S(1)}, bf16[768,384]{1,0:T(8,128)(2,1)S(1)}, u32[]{:S(2)}, u32[]{:S(2)}) collective-permute-start(bf16[768,384]{1,0:T(8,128)(2,1)S(1)} %collective-permute-done.8), channel_id=1, source_target_pairs={{0,112},{16,0},{32,16},{48,32},{64,48},{80,64},{96,80},{112,96},{1... | collective-permute-start | bytes 1769480 | tf_op jit(solution)/shard_map/ppermute | solution.py:25
  266.9 10.5 %collective-permute-start.11 = (bf16[768,384]{1,0:T(8,128)(2,1)S(1)}, bf16[768,384]{1,0:T(8,128)(2,1)S(1)}, u32[]{:S(2)}, u32[]{:S(2)}) collective-permute-start(bf16[768,384]{1,0:T(8,128)(2,1)S(1)} %collective-permute-done.9), channel_id=1, source_target_pairs={{0,16},{16,32},{32,48},{48,64},{64,80},{80,96},{96,112},{112,0},{1... | collective-permute-start | bytes 1769480 | tf_op jit(solution)/shard_map/ppermute | solution.py:20
  266.9 14.1 %collective-permute-start.12 = (bf16[768,384]{1,0:T(8,128)(2,1)S(1)}, bf16[768,384]{1,0:T(8,128)(2,1)S(1)}, u32[]{:S(2)}, u32[]{:S(2)}) collective-permute-start(bf16[768,384]{1,0:T(8,128)(2,1)S(1)} %collective-permute-done.10), channel_id=1, source_target_pairs={{0,112},{16,0},{32,16},{48,32},{64,48},{80,64},{96,80},{112,96},{1... | collective-permute-start | bytes 1769480 | tf_op jit(solution)/shard_map/ppermute | solution.py:25
  277.4 10.5 %collective-permute-start.13 = (bf16[768,384]{1,0:T(8,128)(2,1)S(1)}, bf16[768,384]{1,0:T(8,128)(2,1)S(1)}, u32[]{:S(2)}, u32[]{:S(2)}) collective-permute-start(bf16[768,384]{1,0:T(8,128)(2,1)S(1)} %collective-permute-done.11), channel_id=1, source_target_pairs={{0,16},{16,32},{32,48},{48,64},{64,80},{80,96},{96,112},{112,0},{1... | collective-permute-start | bytes 1769480 | tf_op jit(solution)/shard_map/ppermute | solution.py:20
  352.1 85.2 %copy-start.5 = (bf16[768,384]{1,0:T(8,128)(2,1)S(1)}, bf16[768,384]{1,0:T(8,128)(2,1)}, u32[]{:S(2)}) copy-start(bf16[768,384]{1,0:T(8,128)(2,1)} %get-tuple-element.9) | copy-start | bytes 1769476
  427.9 9.4 %copy-start.6 = (bf16[768,6144]{1,0:T(8,128)(2,1)S(1)}, bf16[768,6144]{1,0:T(8,128)(2,1)}, u32[]{:S(2)}) copy-start(bf16[768,6144]{1,0:T(8,128)(2,1)} %all-gather.11.cloned.1.call-done) | copy-start | bytes 28311556
Sparse Core Ops, SparseCore 0:
  9.7 38.0 all-gather.8
  49.9 88.6 all-gather.6
  140.8 74.9 all-gather.14
  217.8 37.9 all-gather.12
  258.3 83.8 all-gather.10
  344.8 83.0 all-gather.16
